TPU v7x, 32 devices: a whole 2x2x4 slice. The times are simulated.
32 devices in a mesh: dp: 8 (over z, x), ctx: 4 (over y, core).
Axes of the slice: x: 2, y: 2, z: 4, core: 2. Of those that a mesh axis runs over, the one named last changes fastest.
Arguments:
- queries: bfloat16 [8, 4, 2, 64, 2048], P('dp', 'ctx'), may hold values from -6 to 6
- keys: bfloat16 [8, 4, 2, 64, 512], P('dp', 'ctx'), may hold values from -6 to 6
- values: bfloat16 [8, 4, 2, 64, 512], P('dp', 'ctx'), may hold values from -6 to 6
- out_grad: bfloat16 [8, 4, 2, 64, 2048], P('dp', 'ctx'), may hold values from -6 to 6
- layer_input: bfloat16 [8, 4, 2, 64, 4096], P('dp', 'ctx'), may hold values from -6 to 6
- doc_lengths: int32 [8, 16], P('dp'), may hold values from 1 to 64, as said below
Outputs:
- query_grad: bfloat16 [8, 4, 2, 64, 2048], P('dp', 'ctx')
- key_grad: bfloat16 [8, 4, 2, 64, 512], P('dp', 'ctx')
- value_grad: bfloat16 [8, 4, 2, 64, 512], P('dp', 'ctx')
- weight_grad: float32 [4096, 512], P('ctx', 'dp')
Inputs may be any that keep to these rules, and one draw needn't show every extreme that they name: `doc_lengths`: each sequence is 16 documents laid end to end that fill its 512 tokens; no document is longer than 64 tokens, and one of each sequence has exactly 64.
All inputs are finite; a program needn't handle non-finite values.
Results may differ from a plain program's by a relative error of at most 0.03.
Values may be sent and summed in bfloat16 or wider, within the bound.
A program may use at most 64 MiB of HBM per device.

v0:
```python
import functools
import math

import jax
import jax.numpy as jnp
from jax import lax
from jax.experimental import pallas as pl
from jax.experimental.pallas import tpu as pltpu
from jax.sharding import PartitionSpec as P

HD = 128
MESH = pl.DeviceIdType.MESH
VMEM_LIMIT = 63 * 1024 * 1024


def dot(a, b, ca, cb):
    return lax.dot_general(a, b, (((ca,), (cb,)), ((), ())), preferred_element_type=jnp.float32)


def kernel(
    n_ctx, n_hi, n_lo, span, kvh, groups,
    q_hbm, k_hbm, v_hbm, g_hbm, li_ref, len_hbm,
    dq_hbm, dk_hbm, dv_hbm, w_hbm,
    dq_ref, dk_ref, dv_ref, w_ref, out_sem,
    q_ref, g_ref, len_ref, kv, sent, back, own, li_buf, vg_buf, part, recv_lo, part_hi, recv_hi,
    in_sem, kv_sem, fold_sem, halo_ss, halo_rs, back_ss, back_rs, li_ss, li_rs, li_own,
    pair_ss, pair_rs, vg_ss, vg_rs, fwd_ss, fwd_rs, lo_ss, lo_rs, hi_ss, hi_rs,
):
    me = lax.axis_index("ctx")
    place = lax.axis_index("dp")
    my_hi = place // n_lo
    my_lo = place % n_lo
    last = n_ctx - 1
    tokens = 2 * span
    chunk = li_buf.shape[1]
    pieces, _, blk, width = part.shape[1:]
    inverse_root = 1.0 / math.sqrt(HD)

    def ctx_id(i):
        return (place, i)

    def dp_id(d):
        return (d, me)

    partner = me + 1 - 2 * lax.rem(me, 2)
    same_core = [lax.rem(me + 2 * j, n_ctx) for j in range(1, n_ctx // 2)]
    ctx_peers = [lax.rem(me + j, n_ctx) for j in range(1, n_ctx)]
    lo_peers = [lax.rem(my_lo + j, n_lo) for j in range(1, n_lo)]
    hi_peers = [lax.rem(my_hi + j, n_hi) for j in range(1, n_hi)]

    locals_in = [
        pltpu.make_async_copy(len_hbm, len_ref, in_sem.at[0]),
        pltpu.make_async_copy(q_hbm, q_ref, in_sem.at[1]),
        pltpu.make_async_copy(g_hbm, g_ref, in_sem.at[2]),
    ]
    own_kv = [
        pltpu.make_async_copy(
            source.at[pl.ds(slot * span, span)],
            kv.at[slot, which, pl.ds(span, span)],
            kv_sem.at[slot, which],
        )
        for slot in range(2)
        for which, source in enumerate((k_hbm, v_hbm))
    ]
    fold_kv = [
        pltpu.make_async_copy(
            source.at[pl.ds(0, span)], kv.at[1, which, pl.ds(0, span)], fold_sem.at[which]
        )
        for which, source in enumerate((k_hbm, v_hbm))
    ]
    my_rows = pl.ds(pl.multiple_of(me * tokens, tokens), tokens)
    li_local = pltpu.make_async_copy(
        li_ref.at[:, pl.ds(pl.multiple_of(me * chunk, chunk), chunk)], li_buf.at[my_rows], li_own
    )
    for copy in own_kv + locals_in:
        copy.start()

    barrier = pltpu.get_barrier_semaphore()
    for peer in ctx_peers:
        pl.semaphore_signal(barrier, inc=1, device_id=ctx_id(peer), device_id_type=MESH)
    for peer in lo_peers:
        pl.semaphore_signal(barrier, inc=1, device_id=dp_id(my_hi * n_lo + peer), device_id_type=MESH)
    for peer in hi_peers:
        pl.semaphore_signal(barrier, inc=1, device_id=dp_id(peer * n_lo + my_lo), device_id_type=MESH)

    @pl.when(me == 0)
    def _():
        kv[0, :, pl.ds(0, span)] = jnp.zeros((2, span, kv.shape[3]), kv.dtype)
        back[1] = jnp.zeros(back.shape[1:], back.dtype)

    @pl.when(me == last)
    def _():
        for copy in fold_kv:
            copy.start()

    pl.semaphore_wait(barrier, n_ctx + n_lo + n_hi - 3)

    def halo_copy(slot, which):
        source = (k_hbm, v_hbm)[which]
        return pltpu.make_async_remote_copy(
            src_ref=source.at[pl.ds(slot * span, span)],
            dst_ref=kv.at[slot, which, pl.ds(0, span)],
            send_sem=halo_ss.at[slot, which],
            recv_sem=halo_rs.at[slot, which],
            device_id=ctx_id(jnp.minimum(me + 1, last) if slot == 0 else jnp.maximum(me - 1, 0)),
            device_id_type=MESH,
        )

    def back_copy(slot):
        return pltpu.make_async_remote_copy(
            src_ref=sent.at[slot],
            dst_ref=back.at[slot],
            send_sem=back_ss.at[slot],
            recv_sem=back_rs.at[slot],
            device_id=ctx_id(jnp.maximum(me - 1, 0) if slot == 0 else jnp.minimum(me + 1, last)),
            device_id_type=MESH,
        )

    @pl.when(me < last)
    def _():
        for which in range(2):
            halo_copy(0, which).start()

    @pl.when(me > 0)
    def _():
        for which in range(2):
            halo_copy(1, which).start()

    def li_copy(j):
        peer = ctx_peers[j]
        return pltpu.make_async_remote_copy(
            src_ref=li_ref.at[:, pl.ds(pl.multiple_of(peer * chunk, chunk), chunk)],
            dst_ref=li_buf.at[my_rows],
            send_sem=li_ss.at[j],
            recv_sem=li_rs.at[j],
            device_id=ctx_id(peer),
            device_id_type=MESH,
        )

    for j in range(n_ctx - 1):
        li_copy(j).start()
    li_local.start()
    for copy in own_kv + locals_in:
        copy.wait()

    for slot in range(2):
        stretch = me if slot == 0 else 2 * n_ctx - 1 - me
        first = stretch * span
        lane = lax.broadcasted_iota(jnp.int32, (1, groups * span), 1)
        pos = first + lax.rem(lane, span)
        begin = jnp.zeros_like(pos)
        run = jnp.int32(0)
        for j in range(len_ref.shape[1]):
            begin = jnp.where(pos >= run, run, begin)
            run = run + len_ref[0, j]
        key_pos = first - span + lax.broadcasted_iota(jnp.int32, (2 * span, groups * span), 0)
        allowed = (key_pos >= begin) & (key_pos <= pos)

        @pl.when((me > 0) if slot == 0 else (me < last))
        def _():
            for which in range(2):
                halo_copy(slot, which).wait_recv()

        if slot == 1:
            @pl.when(me == last)
            def _():
                for copy in fold_kv:
                    copy.wait()

        rows = pl.ds(slot * span, span)
        for g in range(kvh):
            col = slice(g * HD, (g + 1) * HD)
            heads = [slice(h * HD, (h + 1) * HD) for h in range(g * groups, (g + 1) * groups)]
            kk = kv[slot, 0, :, col]
            vv = kv[slot, 1, :, col]
            qq = jnp.concatenate([q_ref[rows, h] for h in heads], axis=0)
            gg = jnp.concatenate([g_ref[rows, h] for h in heads], axis=0)
            scores = jnp.where(allowed, dot(kk, qq, 1, 1) * inverse_root, -1e30)
            weights = jnp.exp(scores - jnp.max(scores, axis=0, keepdims=True))
            probs = weights * (1.0 / jnp.sum(weights, axis=0, keepdims=True))
            low = probs.astype(jnp.bfloat16)
            dprob = dot(vv, gg, 1, 1)
            delta = jnp.sum(low.astype(jnp.float32) * dprob, axis=0, keepdims=True)
            ds = (probs * (dprob - delta)).astype(jnp.bfloat16)
            dk = dot(ds, qq, 1, 0) * inverse_root
            dv = dot(low, gg, 1, 0)
            dq = (dot(ds, kk, 0, 0) * inverse_root).astype(jnp.bfloat16)
            for n, h in enumerate(heads):
                dq_ref[rows, h] = dq[n * span : (n + 1) * span]
            sent[slot, 0, :, col] = dk[:span].astype(jnp.bfloat16)
            sent[slot, 1, :, col] = dv[:span].astype(jnp.bfloat16)
            own[slot, 0, :, col] = dk[span:]
            own[slot, 1, :, col] = dv[span:]

        @pl.when((me > 0) if slot == 0 else (me < last))
        def _():
            back_copy(slot).start()

    outs = [
        pltpu.make_async_copy(dq_ref, dq_hbm, out_sem.at[0]),
        pltpu.make_async_copy(dv_ref, dv_hbm, out_sem.at[1]),
        pltpu.make_async_copy(dk_ref, dk_hbm, out_sem.at[2]),
        pltpu.make_async_copy(w_ref, w_hbm, out_sem.at[3]),
    ]
    outs[0].start()

    @pl.when(me == last)
    def _():
        back[0] = sent[1]

    for slot in range(2):
        @pl.when((me < last) if slot == 0 else (me > 0))
        def _():
            back_copy(slot).wait_recv()

        rows = pl.ds(slot * span, span)
        dv_ref[rows] = (own[slot, 1] + back[slot, 1].astype(jnp.float32)).astype(jnp.bfloat16)

    def columns(i):
        return pl.ds(pl.multiple_of(i * tokens, tokens), tokens)

    def vg_send(source, target, send_sem, recv_sem):
        return pltpu.make_async_remote_copy(
            src_ref=vg_buf.at[:, columns(source)],
            dst_ref=vg_buf.at[:, columns(source)],
            send_sem=send_sem,
            recv_sem=recv_sem,
            device_id=ctx_id(target),
            device_id_type=MESH,
        )

    vg_buf[:, columns(me)] = dv_ref[...].T
    far = range(n_ctx // 2 - 1)
    for j in far:
        vg_send(me, same_core[j], vg_ss.at[j], vg_rs.at[j]).start()
    pair = vg_send(me, partner, pair_ss, pair_rs)
    pair.start()
    for slot in range(2):
        rows = pl.ds(slot * span, span)
        dk_ref[rows] = (own[slot, 0] + back[slot, 0].astype(jnp.float32)).astype(jnp.bfloat16)
    outs[1].start()
    outs[2].start()
    li_local.wait()
    for j in range(n_ctx - 1):
        li_copy(j).wait_recv()

    def forward(j):
        source = lax.rem(me - 2 * (j + 1) + n_ctx, n_ctx)
        return vg_send(source, partner, fwd_ss.at[j], fwd_rs.at[j])

    for j in far:
        vg_send(me, same_core[j], vg_ss.at[j], vg_rs.at[j]).wait_recv()
        forward(j).start()
    pair.wait_recv()
    for j in far:
        forward(j).wait_recv()

    def lo_copy(c, j):
        peer = lo_peers[j]
        return pltpu.make_async_remote_copy(
            src_ref=part.at[peer, c],
            dst_ref=recv_lo.at[j, c],
            send_sem=lo_ss.at[j, c],
            recv_sem=lo_rs.at[j, c],
            device_id=dp_id(my_hi * n_lo + peer),
            device_id_type=MESH,
        )

    for c in range(pieces):
        product = dot(vg_buf[...], li_buf[:, c * width : (c + 1) * width], 1, 0)
        for h in range(n_hi):
            for l in range(n_lo):
                top = (h * n_lo + l) * blk
                part[l, c, h] = product[top : top + blk].astype(jnp.bfloat16)
        for j in range(n_lo - 1):
            lo_copy(c, j).start()

    def hi_copy(c, j):
        return pltpu.make_async_remote_copy(
            src_ref=part_hi.at[c, hi_peers[j]],
            dst_ref=recv_hi.at[c, j],
            send_sem=hi_ss.at[c, j],
            recv_sem=hi_rs.at[c, j],
            device_id=dp_id(hi_peers[j] * n_lo + my_lo),
            device_id_type=MESH,
        )

    for c in range(pieces):
        for j in range(n_lo - 1):
            lo_copy(c, j).wait_recv()
        total = part[my_lo, c].astype(jnp.float32)
        for j in range(n_lo - 1):
            total = total + recv_lo[j, c].astype(jnp.float32)
        part_hi[c] = total.astype(jnp.bfloat16)
        for j in range(n_hi - 1):
            hi_copy(c, j).start()

    for c in range(pieces):
        total = part[my_lo, c, my_hi].astype(jnp.float32)
        for j in range(n_lo - 1):
            total = total + recv_lo[j, c, my_hi].astype(jnp.float32)
        for j in range(n_hi - 1):
            hi_copy(c, j).wait_recv()
            total = total + recv_hi[c, j].astype(jnp.float32)
        w_ref[:, c * width : (c + 1) * width] = total * (1.0 / (n_hi * n_lo))
    outs[3].start()

    @pl.when(me < last)
    def _():
        for which in range(2):
            halo_copy(0, which).wait_send()
        back_copy(1).wait_send()

    @pl.when(me > 0)
    def _():
        for which in range(2):
            halo_copy(1, which).wait_send()
        back_copy(0).wait_send()

    for j in range(n_ctx - 1):
        li_copy(j).wait_send()
    pair.wait_send()
    for j in far:
        vg_send(me, same_core[j], vg_ss.at[j], vg_rs.at[j]).wait_send()
        forward(j).wait_send()
    for c in range(pieces):
        for j in range(n_lo - 1):
            lo_copy(c, j).wait_send()
        for j in range(n_hi - 1):
            hi_copy(c, j).wait_send()
    for copy in outs:
        copy.wait()


def hand_over(*refs):
    count = len(refs) // 3
    sem = refs[-1]
    fetch = [pltpu.make_async_copy(refs[n], refs[2 * count + n], sem.at[0, n]) for n in range(count)]
    store = [
        pltpu.make_async_copy(refs[2 * count + n], refs[count + n], sem.at[1, n])
        for n in range(count)
    ]
    for copy in fetch:
        copy.start()
    for n in range(count):
        fetch[n].wait()
        store[n].start()
    for copy in store:
        copy.wait()


def body(n_ctx, n_dp, queries, keys, values, out_grad, layer_input, doc_lengths):
    span = queries.shape[3]
    tokens = 2 * span
    q = queries.reshape(tokens, queries.shape[4])
    k = keys.reshape(tokens, keys.shape[4])
    v = values.reshape(tokens, values.shape[4])
    g = out_grad.reshape(tokens, out_grad.shape[4])
    li = layer_input.reshape(tokens, layer_input.shape[4])
    kv_width = k.shape[1]
    kvh = kv_width // HD
    groups = q.shape[1] // kv_width
    chunk = li.shape[1] // n_ctx
    blk = kv_width // n_dp
    n_lo = 2 ** ((n_dp.bit_length() - 1) // 2)
    n_hi = n_dp // n_lo
    width = min(256, chunk)
    pieces = chunk // width
    far = max(1, n_ctx // 2 - 1)
    bf16, f32 = jnp.bfloat16, jnp.float32
    dma = pltpu.SemaphoreType.DMA
    hbm = pl.BlockSpec(memory_space=pltpu.HBM)
    shapes = (
        jax.ShapeDtypeStruct(q.shape, bf16),
        jax.ShapeDtypeStruct(k.shape, bf16),
        jax.ShapeDtypeStruct(v.shape, bf16),
        jax.ShapeDtypeStruct((blk, chunk), f32),
    )
    outs = pl.pallas_call(
        functools.partial(kernel, n_ctx, n_hi, n_lo, span, kvh, groups),
        out_shape=shapes,
        in_specs=[hbm] * 6,
        out_specs=(hbm,) * 4,
        scratch_shapes=[
            pltpu.VMEM(q.shape, bf16),
            pltpu.VMEM(k.shape, bf16),
            pltpu.VMEM(v.shape, bf16),
            pltpu.VMEM((blk, chunk), f32),
            dma((4,)),
            pltpu.VMEM(q.shape, bf16),
            pltpu.VMEM(g.shape, bf16),
            pltpu.SMEM(doc_lengths.shape, jnp.int32),
            pltpu.VMEM((2, 2, 2 * span, kv_width), bf16),
            pltpu.VMEM((2, 2, span, kv_width), bf16),
            pltpu.VMEM((2, 2, span, kv_width), bf16),
            pltpu.VMEM((2, 2, span, kv_width), f32),
            pltpu.VMEM((n_ctx * tokens, chunk), bf16),
            pltpu.VMEM((kv_width, n_ctx * tokens), bf16),
            pltpu.VMEM((n_lo, pieces, n_hi, blk, width), bf16),
            pltpu.VMEM((n_lo - 1, pieces, n_hi, blk, width), bf16),
            pltpu.VMEM((pieces, n_hi, blk, width), bf16),
            pltpu.VMEM((pieces, n_hi - 1, blk, width), bf16),
            dma((3,)), dma((2, 2)), dma((2,)),
            dma((2, 2)), dma((2, 2)), dma((2,)), dma((2,)),
            dma((n_ctx - 1,)), dma((n_ctx - 1,)), dma,
            dma, dma, dma((far,)), dma((far,)), dma((far,)), dma((far,)),
            dma((n_lo - 1, pieces)), dma((n_lo - 1, pieces)),
            dma((pieces, n_hi - 1)), dma((pieces, n_hi - 1)),
        ],
        compiler_params=pltpu.CompilerParams(
            collective_id=0, has_side_effects=True, vmem_limit_bytes=VMEM_LIMIT
        ),
        name="attention_grads",
    )(q, k, v, g, li, doc_lengths)
    dq, dk, dv, w = pl.pallas_call(
        hand_over,
        out_shape=shapes,
        in_specs=[hbm] * 4,
        out_specs=(hbm,) * 4,
        scratch_shapes=[pltpu.VMEM(out.shape, out.dtype) for out in shapes] + [dma((2, 4))],
        compiler_params=pltpu.CompilerParams(vmem_limit_bytes=VMEM_LIMIT),
        name="hand_over",
    )(*outs)
    return (
        dq.reshape(queries.shape),
        dk.reshape(keys.shape),
        dv.reshape(values.shape),
        w.T,
    )


def solution(mesh):
    tokens = P("dp", "ctx", None, None, None)
    return jax.shard_map(
        functools.partial(body, mesh.shape["ctx"], mesh.shape["dp"]),
        mesh=mesh,
        in_specs=(tokens, tokens, tokens, tokens, tokens, P("dp", None)),
        out_specs=(tokens, tokens, tokens, P("ctx", "dp")),
        check_vma=False,
    )
```

profile of v0, /device:TPU:0, one launch (start us, length us, event | category | flops | bytes accessed | tf_op | source)
XLA Modules:
  0.0 48.8 jit_solution(7100562747757697840)
XLA Ops:
  0.6 46.1 %attention_grads.1 = (bf16[128,2048]{1,0:T(8,128)(2,1)}, bf16[128,512]{1,0:T(8,128)(2,1)}, bf16[128,512]{1,0:T(8,128)(2,1)}, f32[64,1024]{1,0:T(8,128)}) custom-call(bf16[128,2048]{1,0:T(8,128)(2,1)} %bitcast.10, bf16[128,512]{1,0:T(8,128)(2,1)} %bitcast.12, bf16[128,512]{1,0:T(8,128)(2,1)} %bitcast.13, bf16[128,2048]{1,0:T(8,128)(2,1)} %bitcast.11, ...), custom_call_target="tpu_custom_call" | custom-call | tf_op jit(solution)/shard_map/attention_grads/pallas_call | solution.py:379
  46.7 2.1 %hand_over.1 = (bf16[128,2048]{1,0:T(8,128)(2,1)}, bf16[128,512]{1,0:T(8,128)(2,1)}, bf16[128,512]{1,0:T(8,128)(2,1)}, f32[64,1024]{1,0:T(8,128)}) custom-call(bf16[128,2048]{1,0:T(8,128)(2,1)} %get-tuple-element.12.refs_0_, bf16[128,512]{1,0:T(8,128)(2,1)} %get-tuple-element.13.refs_1_, bf16[128,512]{1,0:T(8,128)(2,1)} %get-tuple-element.14.refs_2_, ...), custom_call_target="tpu_custom_call" | custom-call | tf_op jit(solution)/shard_map/hand_over/pallas_call | solution.py:415
where the time goes:
time: 49 us; the launch traced here: 48.8 us
  Pallas kernels  48.2 us (98%)
  between operations  0.64 us (1%)
    pallas_call x1, Pallas kernels, body(): pl.pallas_call(functools.partial(kernel, n_ctx, n_hi, n_lo, span, kvh, gr...  46.1 us
    pallas_call x1, Pallas kernels, body(): pl.pallas_call(hand_over, out_shape=shapes, in_specs=[hbm] * 4, out_specs...  2.07 us

commit v1 on v0

--- a/solution.py
+++ b/solution.py
@@ -86,7 +86,8 @@
     @pl.when(me == 0)
     def _():
         kv[0, :, pl.ds(0, span)] = jnp.zeros((2, span, kv.shape[3]), kv.dtype)
-        back[1] = jnp.zeros(back.shape[1:], back.dtype)
+        for g in range(kvh):
+            back[g, 1] = jnp.zeros(back.shape[2:], back.dtype)
 
     @pl.when(me == last)
     def _():
@@ -106,12 +107,12 @@
             device_id_type=MESH,
         )
 
-    def back_copy(slot):
-        return pltpu.make_async_remote_copy(
-            src_ref=sent.at[slot],
-            dst_ref=back.at[slot],
-            send_sem=back_ss.at[slot],
-            recv_sem=back_rs.at[slot],
+    def back_copy(g, slot):
+        return pltpu.make_async_remote_copy(
+            src_ref=sent.at[g, slot],
+            dst_ref=back.at[g, slot],
+            send_sem=back_ss.at[g, slot],
+            recv_sem=back_rs.at[g, slot],
             device_id=ctx_id(jnp.maximum(me - 1, 0) if slot == 0 else jnp.minimum(me + 1, last)),
             device_id_type=MESH,
         )
@@ -143,6 +144,7 @@
     for copy in own_kv + locals_in:
         copy.wait()
 
+    masks = []
     for slot in range(2):
         stretch = me if slot == 0 else 2 * n_ctx - 1 - me
         first = stretch * span
@@ -154,28 +156,53 @@
             begin = jnp.where(pos >= run, run, begin)
             run = run + len_ref[0, j]
         key_pos = first - span + lax.broadcasted_iota(jnp.int32, (2 * span, groups * span), 0)
-        allowed = (key_pos >= begin) & (key_pos <= pos)
+        masks.append((key_pos >= begin) & (key_pos <= pos))
 
         @pl.when((me > 0) if slot == 0 else (me < last))
         def _():
             for which in range(2):
                 halo_copy(slot, which).wait_recv()
 
-        if slot == 1:
-            @pl.when(me == last)
-            def _():
-                for copy in fold_kv:
-                    copy.wait()
-
-        rows = pl.ds(slot * span, span)
-        for g in range(kvh):
-            col = slice(g * HD, (g + 1) * HD)
-            heads = [slice(h * HD, (h + 1) * HD) for h in range(g * groups, (g + 1) * groups)]
+    @pl.when(me == last)
+    def _():
+        for copy in fold_kv:
+            copy.wait()
+
+    def columns(i):
+        return pl.ds(pl.multiple_of(i * tokens, tokens), tokens)
+
+    def vg_send(g, source, target, send_sem, recv_sem):
+        return pltpu.make_async_remote_copy(
+            src_ref=vg_buf.at[pl.ds(g * HD, HD), columns(source)],
+            dst_ref=vg_buf.at[pl.ds(g * HD, HD), columns(source)],
+            send_sem=send_sem,
+            recv_sem=recv_sem,
+            device_id=ctx_id(target),
+            device_id_type=MESH,
+        )
+
+    far = range(n_ctx // 2 - 1)
+
+    def over(g, j):
+        return vg_send(g, me, same_core[j], vg_ss.at[g, j], vg_rs.at[g, j])
+
+    def pair(g):
+        return vg_send(g, me, partner, pair_ss.at[g], pair_rs.at[g])
+
+    def forward(g, j):
+        source = lax.rem(me - 2 * (j + 1) + n_ctx, n_ctx)
+        return vg_send(g, source, partner, fwd_ss.at[g, j], fwd_rs.at[g, j])
+
+    def attend(g):
+        col = slice(g * HD, (g + 1) * HD)
+        heads = [slice(h * HD, (h + 1) * HD) for h in range(g * groups, (g + 1) * groups)]
+        for slot in range(2):
+            rows = pl.ds(slot * span, span)
             kk = kv[slot, 0, :, col]
             vv = kv[slot, 1, :, col]
             qq = jnp.concatenate([q_ref[rows, h] for h in heads], axis=0)
             gg = jnp.concatenate([g_ref[rows, h] for h in heads], axis=0)
-            scores = jnp.where(allowed, dot(kk, qq, 1, 1) * inverse_root, -1e30)
+            scores = jnp.where(masks[slot], dot(kk, qq, 1, 1) * inverse_root, -1e30)
             weights = jnp.exp(scores - jnp.max(scores, axis=0, keepdims=True))
             probs = weights * (1.0 / jnp.sum(weights, axis=0, keepdims=True))
             low = probs.astype(jnp.bfloat16)
@@ -187,14 +214,58 @@
             dq = (dot(ds, kk, 0, 0) * inverse_root).astype(jnp.bfloat16)
             for n, h in enumerate(heads):
                 dq_ref[rows, h] = dq[n * span : (n + 1) * span]
-            sent[slot, 0, :, col] = dk[:span].astype(jnp.bfloat16)
-            sent[slot, 1, :, col] = dv[:span].astype(jnp.bfloat16)
+            sent[g, slot, 0] = dk[:span].astype(jnp.bfloat16)
+            sent[g, slot, 1] = dv[:span].astype(jnp.bfloat16)
             own[slot, 0, :, col] = dk[span:]
             own[slot, 1, :, col] = dv[span:]
 
-        @pl.when((me > 0) if slot == 0 else (me < last))
-        def _():
-            back_copy(slot).start()
+        @pl.when(me > 0)
+        def _():
+            back_copy(g, 0).start()
+
+        @pl.when(me < last)
+        def _():
+            back_copy(g, 1).start()
+
+        @pl.when(me == last)
+        def _():
+            back[g, 0] = sent[g, 1]
+
+    def settle(g):
+        @pl.when(me < last)
+        def _():
+            back_copy(g, 0).wait_recv()
+
+        @pl.when(me > 0)
+        def _():
+            back_copy(g, 1).wait_recv()
+
+        col = slice(g * HD, (g + 1) * HD)
+        for slot in range(2):
+            rows = pl.ds(slot * span, span)
+            dv_ref[rows, col] = (own[slot, 1, :, col] + back[g, slot, 1].astype(jnp.float32)).astype(
+                jnp.bfloat16
+            )
+        vg_buf[pl.ds(g * HD, HD), columns(me)] = dv_ref[:, col].T
+        for j in far:
+            over(g, j).start()
+        pair(g).start()
+        for slot in range(2):
+            rows = pl.ds(slot * span, span)
+            dk_ref[rows, col] = (own[slot, 0, :, col] + back[g, slot, 0].astype(jnp.float32)).astype(
+                jnp.bfloat16
+            )
+
+    def pass_on(g):
+        for j in far:
+            over(g, j).wait_recv()
+            forward(g, j).start()
+
+    for g in range(kvh):
+        attend(g)
+        if g >= 1:
+            settle(g - 1)
+    settle(kvh - 1)
 
     outs = [
         pltpu.make_async_copy(dq_ref, dq_hbm, out_sem.at[0]),
@@ -204,56 +275,17 @@
     ]
     outs[0].start()
 
-    @pl.when(me == last)
-    def _():
-        back[0] = sent[1]
-
-    for slot in range(2):
-        @pl.when((me < last) if slot == 0 else (me > 0))
-        def _():
-            back_copy(slot).wait_recv()
-
-        rows = pl.ds(slot * span, span)
-        dv_ref[rows] = (own[slot, 1] + back[slot, 1].astype(jnp.float32)).astype(jnp.bfloat16)
-
-    def columns(i):
-        return pl.ds(pl.multiple_of(i * tokens, tokens), tokens)
-
-    def vg_send(source, target, send_sem, recv_sem):
-        return pltpu.make_async_remote_copy(
-            src_ref=vg_buf.at[:, columns(source)],
-            dst_ref=vg_buf.at[:, columns(source)],
-            send_sem=send_sem,
-            recv_sem=recv_sem,
-            device_id=ctx_id(target),
-            device_id_type=MESH,
-        )
-
-    vg_buf[:, columns(me)] = dv_ref[...].T
-    far = range(n_ctx // 2 - 1)
-    for j in far:
-        vg_send(me, same_core[j], vg_ss.at[j], vg_rs.at[j]).start()
-    pair = vg_send(me, partner, pair_ss, pair_rs)
-    pair.start()
-    for slot in range(2):
-        rows = pl.ds(slot * span, span)
-        dk_ref[rows] = (own[slot, 0] + back[slot, 0].astype(jnp.float32)).astype(jnp.bfloat16)
     outs[1].start()
     outs[2].start()
+    for g in range(kvh):
+        pass_on(g)
     li_local.wait()
     for j in range(n_ctx - 1):
         li_copy(j).wait_recv()
-
-    def forward(j):
-        source = lax.rem(me - 2 * (j + 1) + n_ctx, n_ctx)
-        return vg_send(source, partner, fwd_ss.at[j], fwd_rs.at[j])
-
-    for j in far:
-        vg_send(me, same_core[j], vg_ss.at[j], vg_rs.at[j]).wait_recv()
-        forward(j).start()
-    pair.wait_recv()
-    for j in far:
-        forward(j).wait_recv()
+    for g in range(kvh):
+        pair(g).wait_recv()
+        for j in far:
+            forward(g, j).wait_recv()
 
     def lo_copy(c, j):
         peer = lo_peers[j]
@@ -309,20 +341,23 @@
     def _():
         for which in range(2):
             halo_copy(0, which).wait_send()
-        back_copy(1).wait_send()
+        for g in range(kvh):
+            back_copy(g, 1).wait_send()
 
     @pl.when(me > 0)
     def _():
         for which in range(2):
             halo_copy(1, which).wait_send()
-        back_copy(0).wait_send()
+        for g in range(kvh):
+            back_copy(g, 0).wait_send()
 
     for j in range(n_ctx - 1):
         li_copy(j).wait_send()
-    pair.wait_send()
-    for j in far:
-        vg_send(me, same_core[j], vg_ss.at[j], vg_rs.at[j]).wait_send()
-        forward(j).wait_send()
+    for g in range(kvh):
+        pair(g).wait_send()
+        for j in far:
+            over(g, j).wait_send()
+            forward(g, j).wait_send()
     for c in range(pieces):
         for j in range(n_lo - 1):
             lo_copy(c, j).wait_send()
@@ -391,8 +426,8 @@
             pltpu.VMEM(g.shape, bf16),
             pltpu.SMEM(doc_lengths.shape, jnp.int32),
             pltpu.VMEM((2, 2, 2 * span, kv_width), bf16),
-            pltpu.VMEM((2, 2, span, kv_width), bf16),
-            pltpu.VMEM((2, 2, span, kv_width), bf16),
+            pltpu.VMEM((kvh, 2, 2, span, HD), bf16),
+            pltpu.VMEM((kvh, 2, 2, span, HD), bf16),
             pltpu.VMEM((2, 2, span, kv_width), f32),
             pltpu.VMEM((n_ctx * tokens, chunk), bf16),
             pltpu.VMEM((kv_width, n_ctx * tokens), bf16),
@@ -401,9 +436,10 @@
             pltpu.VMEM((pieces, n_hi, blk, width), bf16),
             pltpu.VMEM((pieces, n_hi - 1, blk, width), bf16),
             dma((3,)), dma((2, 2)), dma((2,)),
-            dma((2, 2)), dma((2, 2)), dma((2,)), dma((2,)),
+            dma((2, 2)), dma((2, 2)), dma((kvh, 2)), dma((kvh, 2)),
             dma((n_ctx - 1,)), dma((n_ctx - 1,)), dma,
-            dma, dma, dma((far,)), dma((far,)), dma((far,)), dma((far,)),
+            dma((kvh,)), dma((kvh,)),
+            dma((kvh, far)), dma((kvh, far)), dma((kvh, far)), dma((kvh, far)),
             dma((n_lo - 1, pieces)), dma((n_lo - 1, pieces)),
             dma((pieces, n_hi - 1)), dma((pieces, n_hi - 1)),
         ],

time: 49 us -> 50.7 us (1.035)
  Pallas kernels: 48.2 us -> 49.9 us
    pallas_call x1, Pallas kernels: 46.1 us -> 47.8 us  [body(): pl.pallas_call(functools.partial(kernel, n_ctx, n_hi, n_lo, span, kvh, gr...]
where the time goes in v1:
time: 50.7 us; the launch traced here: 50.5 us
  Pallas kernels  49.9 us (98%)
  between operations  0.64 us (1%)
    pallas_call x1, Pallas kernels, body(): pl.pallas_call(functools.partial(kernel, n_ctx, n_hi, n_lo, span, kvh, gr...  47.8 us
    pallas_call x1, Pallas kernels, body(): pl.pallas_call(hand_over, out_shape=shapes, in_specs=[hbm] * 4, out_specs...  2.07 us

profile of v1, /device:TPU:0, one launch (start us, length us, event | category | flops | bytes accessed | tf_op | source)
XLA Modules:
  0.0 50.5 jit_solution(11574341323581508499)
XLA Ops:
  0.6 47.8 %attention_grads.1 = (bf16[128,2048]{1,0:T(8,128)(2,1)}, bf16[128,512]{1,0:T(8,128)(2,1)}, bf16[128,512]{1,0:T(8,128)(2,1)}, f32[64,1024]{1,0:T(8,128)}) custom-call(bf16[128,2048]{1,0:T(8,128)(2,1)} %bitcast.10, bf16[128,512]{1,0:T(8,128)(2,1)} %bitcast.12, bf16[128,512]{1,0:T(8,128)(2,1)} %bitcast.13, bf16[128,2048]{1,0:T(8,128)(2,1)} %bitcast.11, ...), custom_call_target="tpu_custom_call" | custom-call | tf_op jit(solution)/shard_map/attention_grads/pallas_call | solution.py:414
  48.5 2.1 %hand_over.1 = (bf16[128,2048]{1,0:T(8,128)(2,1)}, bf16[128,512]{1,0:T(8,128)(2,1)}, bf16[128,512]{1,0:T(8,128)(2,1)}, f32[64,1024]{1,0:T(8,128)}) custom-call(bf16[128,2048]{1,0:T(8,128)(2,1)} %get-tuple-element.12.refs_0_, bf16[128,512]{1,0:T(8,128)(2,1)} %get-tuple-element.13.refs_1_, bf16[128,512]{1,0:T(8,128)(2,1)} %get-tuple-element.14.refs_2_, ...), custom_call_target="tpu_custom_call" | custom-call | tf_op jit(solution)/shard_map/hand_over/pallas_call | solution.py:451

commit v2 on v1

--- a/solution.py
+++ b/solution.py
@@ -127,19 +127,21 @@
         for which in range(2):
             halo_copy(1, which).start()
 
-    def li_copy(j):
+    def li_copy(c, j):
         peer = ctx_peers[j]
         return pltpu.make_async_remote_copy(
-            src_ref=li_ref.at[:, pl.ds(pl.multiple_of(peer * chunk, chunk), chunk)],
-            dst_ref=li_buf.at[my_rows],
-            send_sem=li_ss.at[j],
-            recv_sem=li_rs.at[j],
+            src_ref=li_ref.at[:, pl.ds(pl.multiple_of(peer * chunk + c * width, width), width)],
+            dst_ref=li_buf.at[my_rows, pl.ds(c * width, width)],
+            send_sem=li_ss.at[c, j],
+            recv_sem=li_rs.at[c, j],
             device_id=ctx_id(peer),
             device_id_type=MESH,
         )
 
-    for j in range(n_ctx - 1):
-        li_copy(j).start()
+    early = max(1, pieces // 2)
+    for c in range(early):
+        for j in range(n_ctx - 1):
+            li_copy(c, j).start()
     li_local.start()
     for copy in own_kv + locals_in:
         copy.wait()
@@ -266,6 +268,9 @@
         if g >= 1:
             settle(g - 1)
     settle(kvh - 1)
+    for c in range(early, pieces):
+        for j in range(n_ctx - 1):
+            li_copy(c, j).start()
 
     outs = [
         pltpu.make_async_copy(dq_ref, dq_hbm, out_sem.at[0]),
@@ -280,8 +285,6 @@
     for g in range(kvh):
         pass_on(g)
     li_local.wait()
-    for j in range(n_ctx - 1):
-        li_copy(j).wait_recv()
     for g in range(kvh):
         pair(g).wait_recv()
         for j in far:
@@ -298,7 +301,19 @@
             device_id_type=MESH,
         )
 
-    for c in range(pieces):
+    def hi_copy(c, j):
+        return pltpu.make_async_remote_copy(
+            src_ref=part_hi.at[c, hi_peers[j]],
+            dst_ref=recv_hi.at[c, j],
+            send_sem=hi_ss.at[c, j],
+            recv_sem=hi_rs.at[c, j],
+            device_id=dp_id(hi_peers[j] * n_lo + my_lo),
+            device_id_type=MESH,
+        )
+
+    def multiply(c):
+        for j in range(n_ctx - 1):
+            li_copy(c, j).wait_recv()
         product = dot(vg_buf[...], li_buf[:, c * width : (c + 1) * width], 1, 0)
         for h in range(n_hi):
             for l in range(n_lo):
@@ -307,17 +322,7 @@
         for j in range(n_lo - 1):
             lo_copy(c, j).start()
 
-    def hi_copy(c, j):
-        return pltpu.make_async_remote_copy(
-            src_ref=part_hi.at[c, hi_peers[j]],
-            dst_ref=recv_hi.at[c, j],
-            send_sem=hi_ss.at[c, j],
-            recv_sem=hi_rs.at[c, j],
-            device_id=dp_id(hi_peers[j] * n_lo + my_lo),
-            device_id_type=MESH,
-        )
-
-    for c in range(pieces):
+    def reduce(c):
         for j in range(n_lo - 1):
             lo_copy(c, j).wait_recv()
         total = part[my_lo, c].astype(jnp.float32)
@@ -326,6 +331,12 @@
         part_hi[c] = total.astype(jnp.bfloat16)
         for j in range(n_hi - 1):
             hi_copy(c, j).start()
+
+    for c in range(pieces):
+        multiply(c)
+        if c >= 1:
+            reduce(c - 1)
+    reduce(pieces - 1)
 
     for c in range(pieces):
         total = part[my_lo, c, my_hi].astype(jnp.float32)
@@ -351,8 +362,9 @@
         for g in range(kvh):
             back_copy(g, 0).wait_send()
 
-    for j in range(n_ctx - 1):
-        li_copy(j).wait_send()
+    for c in range(pieces):
+        for j in range(n_ctx - 1):
+            li_copy(c, j).wait_send()
     for g in range(kvh):
         pair(g).wait_send()
         for j in far:
@@ -437,7 +449,7 @@
             pltpu.VMEM((pieces, n_hi - 1, blk, width), bf16),
             dma((3,)), dma((2, 2)), dma((2,)),
             dma((2, 2)), dma((2, 2)), dma((kvh, 2)), dma((kvh, 2)),
-            dma((n_ctx - 1,)), dma((n_ctx - 1,)), dma,
+            dma((pieces, n_ctx - 1)), dma((pieces, n_ctx - 1)), dma,
             dma((kvh,)), dma((kvh,)),
             dma((kvh, far)), dma((kvh, far)), dma((kvh, far)), dma((kvh, far)),
             dma((n_lo - 1, pieces)), dma((n_lo - 1, pieces)),

time: 50.7 us -> 45.7 us (0.901)
  Pallas kernels: 49.9 us -> 44.9 us
    pallas_call x1, Pallas kernels: 47.8 us -> 42.8 us  [body(): pl.pallas_call(functools.partial(kernel, n_ctx, n_hi, n_lo, span, kvh, gr...]
where the time goes in v2:
time: 45.7 us; the launch traced here: 45.5 us
  Pallas kernels  44.9 us (98%)
  between operations  0.64 us (1%)
    pallas_call x1, Pallas kernels, body(): pl.pallas_call(functools.partial(kernel, n_ctx, n_hi, n_lo, span, kvh, gr...  42.8 us
    pallas_call x1, Pallas kernels, body(): pl.pallas_call(hand_over, out_shape=shapes, in_specs=[hbm] * 4, out_specs...  2.07 us

profile of v2, /device:TPU:0, one launch (start us, length us, event | category | flops | bytes accessed | tf_op | source)
XLA Modules:
  0.0 45.5 jit_solution(15120738472214510183)
XLA Ops:
  0.6 42.8 %attention_grads.1 = (bf16[128,2048]{1,0:T(8,128)(2,1)}, bf16[128,512]{1,0:T(8,128)(2,1)}, bf16[128,512]{1,0:T(8,128)(2,1)}, f32[64,1024]{1,0:T(8,128)}) custom-call(bf16[128,2048]{1,0:T(8,128)(2,1)} %bitcast.10, bf16[128,512]{1,0:T(8,128)(2,1)} %bitcast.12, bf16[128,512]{1,0:T(8,128)(2,1)} %bitcast.13, bf16[128,2048]{1,0:T(8,128)(2,1)} %bitcast.11, ...), custom_call_target="tpu_custom_call" | custom-call | tf_op jit(solution)/shard_map/attention_grads/pallas_call | solution.py:426
  43.4 2.1 %hand_over.1 = (bf16[128,2048]{1,0:T(8,128)(2,1)}, bf16[128,512]{1,0:T(8,128)(2,1)}, bf16[128,512]{1,0:T(8,128)(2,1)}, f32[64,1024]{1,0:T(8,128)}) custom-call(bf16[128,2048]{1,0:T(8,128)(2,1)} %get-tuple-element.12.refs_0_, bf16[128,512]{1,0:T(8,128)(2,1)} %get-tuple-element.13.refs_1_, bf16[128,512]{1,0:T(8,128)(2,1)} %get-tuple-element.14.refs_2_, ...), custom_call_target="tpu_custom_call" | custom-call | tf_op jit(solution)/shard_map/hand_over/pallas_call | solution.py:463
